TPU v7x, 512 devices: a whole 4x4x16 slice. The times are simulated.
512 devices in a mesh: seq: 64 (over y, z), kvh: 8 (over x, core).
Axes of the slice: x: 4, y: 4, z: 16, core: 2. Of those that a mesh axis runs over, the one named last changes fastest.
Arguments:
- queries: bfloat16 [192, 4, 8192], P('seq', None, 'kvh'), may hold values from -120 to 120
- new_keys: bfloat16 [192, 4, 1024], P('seq', None, 'kvh'), may hold values from -16 to 16
- new_values: bfloat16 [192, 4, 1024], P('seq', None, 'kvh'), may hold values from -6 to 6
- key_cache: bfloat16 [16, 8192, 1024], P(None, 'seq', 'kvh'), may hold values from -6 to 6
- value_cache: bfloat16 [16, 8192, 1024], P(None, 'seq', 'kvh'), may hold values from -6 to 6
- doc_ids: int32 [192], P('seq'), may hold values from 0 to 15
- prefix_len: int32 [192], P('seq'), may hold values from 4097 to 8192
- out_weight: bfloat16 [8192, 8192], P('kvh', 'seq'), may hold values from -0.25 to 0.25
Outputs:
- projected: bfloat16 [192, 4, 8192], P('kvh', None, 'seq')
All inputs are finite; a program needn't handle non-finite values.
Results may differ from a plain program's by a relative error of at most 0.0046.
Values may be sent and summed in bfloat16 or wider, within the bound.
A program may use at most 64 MiB of HBM per device.

v0:
```python
import math

import jax
import jax.numpy as jnp
from jax import lax
from jax.sharding import PartitionSpec as P

HD = 128


masked_score = -1e30


def block_partial(query_block, key_block, value_block, length_block, offset):
    score_scale = 1.0 / math.sqrt(query_block.shape[-1])
    scores = (
        jnp.einsum("rshgd,rthd->rshgt", query_block, key_block, preferred_element_type=jnp.float32)
        * score_scale
    )
    places = offset + jnp.arange(key_block.shape[1], dtype=jnp.int32)
    visible = (places[None, :] < length_block[:, None])[:, None, None, None, :]
    masked = jnp.where(visible, scores, masked_score)
    peak_score = jnp.max(masked, axis=4)
    weights = jnp.where(visible, jnp.exp(masked - peak_score[..., None]), 0.0)
    weight_sum = jnp.sum(weights, axis=4)
    mixture = jnp.einsum(
        "rshgt,rthd->rshgd",
        weights.astype(jnp.bfloat16),
        value_block,
        preferred_element_type=jnp.float32,
    )
    return (peak_score, weight_sum, mixture)


def own_partial(query_view, key_view, value_view):
    score_scale = 1.0 / math.sqrt(query_view.shape[-1])
    scores = (
        jnp.einsum("rshgd,rkhd->rshgk", query_view, key_view, preferred_element_type=jnp.float32)
        * score_scale
    )
    step_count = query_view.shape[1]
    causal = (
        jnp.arange(step_count, dtype=jnp.int32)[None, :]
        <= jnp.arange(step_count, dtype=jnp.int32)[:, None]
    )
    visible = causal[None, :, None, None, :]
    masked = jnp.where(visible, scores, masked_score)
    peak_score = jnp.max(masked, axis=4)
    weights = jnp.where(visible, jnp.exp(masked - peak_score[..., None]), 0.0)
    weight_sum = jnp.sum(weights, axis=4)
    mixture = jnp.einsum(
        "rshgk,rkhd->rshgd",
        weights.astype(jnp.bfloat16),
        value_view,
        preferred_element_type=jnp.float32,
    )
    return (peak_score, weight_sum, mixture)


def merge_pair(first, second):
    peak_first, sum_first, mix_first = first
    peak_second, sum_second, mix_second = second
    peak_top = jnp.maximum(peak_first, peak_second)
    factor_first = jnp.exp(peak_first - peak_top)
    factor_second = jnp.exp(peak_second - peak_top)
    weight_sum = sum_first * factor_first + sum_second * factor_second
    mixture = mix_first * factor_first[..., None] + mix_second * factor_second[..., None]
    return (peak_top, weight_sum, mixture)


def prefix_attend(query_part, doc_ids, prefix_len, key_cache, value_cache):
    local_rows = query_part.shape[0]
    gathered, all_docs, all_lengths = (
        lax.all_gather(query_part, "seq", axis=0, tiled=True),
        lax.all_gather(doc_ids, "seq", axis=0, tiled=True),
        lax.all_gather(prefix_len, "seq", axis=0, tiled=True),
    )
    total_rows, step_count, row_width = gathered.shape
    heads_kv = key_cache.shape[2] // HD
    group_size = row_width // (heads_kv * HD)
    block_rows = 16
    block_count = total_rows // block_rows
    tok_block = key_cache.shape[1]
    offset = lax.axis_index("seq") * tok_block
    query_blocks = gathered.reshape(block_count, block_rows, step_count, heads_kv, group_size, HD)
    doc_blocks = all_docs.reshape(block_count, block_rows)
    length_blocks = all_lengths.reshape(block_count, block_rows)

    def one_block(operands):
        query_block, doc_block, length_block = operands
        key_block = key_cache[doc_block].reshape(block_rows, tok_block, heads_kv, HD)
        value_block = value_cache[doc_block].reshape(block_rows, tok_block, heads_kv, HD)
        return block_partial(query_block, key_block, value_block, length_block, offset)

    peak_parts, sum_parts, mix_parts = lax.map(one_block, (query_blocks, doc_blocks, length_blocks))
    peak_parts = peak_parts.reshape(total_rows, step_count, heads_kv, group_size)
    sum_parts = sum_parts.reshape(total_rows, step_count, heads_kv, group_size)
    mix_parts = mix_parts.reshape(total_rows, step_count, heads_kv, group_size, HD)
    peak_in, sum_in, mix_in = (
        lax.all_to_all(peak_parts, "seq", split_axis=0, concat_axis=0, tiled=True),
        lax.all_to_all(sum_parts, "seq", split_axis=0, concat_axis=0, tiled=True),
        lax.all_to_all(mix_parts, "seq", split_axis=0, concat_axis=0, tiled=True),
    )
    senders = lax.axis_size("seq")
    peak_in = peak_in.reshape(senders, local_rows, step_count, heads_kv, group_size)
    sum_in = sum_in.reshape(senders, local_rows, step_count, heads_kv, group_size)
    mix_in = mix_in.reshape(senders, local_rows, step_count, heads_kv, group_size, HD)
    peak_top = jnp.max(peak_in, axis=0)
    factor = jnp.exp(peak_in - peak_top[None])
    sum_top = jnp.sum(sum_in * factor, axis=0)
    mix_top = jnp.sum(mix_in * factor[..., None], axis=0)
    return (peak_top, sum_top, mix_top)


def shards(queries, new_keys, new_values, key_cache, value_cache, doc_ids, prefix_len, out_weight):
    local_rows, step_count, row_width = queries.shape
    heads_kv = key_cache.shape[2] // HD
    group_size = row_width // (heads_kv * HD)
    prefix_state = prefix_attend(queries, doc_ids, prefix_len, key_cache, value_cache)
    query_view = queries.reshape(local_rows, step_count, heads_kv, group_size, HD)
    own_state = own_partial(
        query_view,
        new_keys.reshape(local_rows, step_count, heads_kv, HD),
        new_values.reshape(local_rows, step_count, heads_kv, HD),
    )
    peak_end, sum_end, mix_end = merge_pair(prefix_state, own_state)
    attention = (
        (mix_end / sum_end[..., None])
        .astype(jnp.bfloat16)
        .reshape(local_rows, step_count, row_width)
    )
    row_piece = lax.all_gather(attention, "seq", axis=0, tiled=True)
    flat_rows = row_piece.reshape(row_piece.shape[0] * step_count, row_width)
    product = jnp.dot(flat_rows, out_weight, preferred_element_type=jnp.float32)
    projected = product.reshape(row_piece.shape[0], step_count, out_weight.shape[1])
    summed = lax.psum_scatter(projected, "kvh", scatter_dimension=0, tiled=True)
    return summed.astype(jnp.bfloat16)


def solution(mesh):
    return jax.shard_map(
        shards,
        mesh=mesh,
        in_specs=(
            P("seq", None, "kvh"),
            P("seq", None, "kvh"),
            P("seq", None, "kvh"),
            P(None, "seq", "kvh"),
            P(None, "seq", "kvh"),
            P("seq"),
            P("seq"),
            P("kvh", "seq"),
        ),
        out_specs=P("kvh", None, "seq"),
        check_vma=False,
    )
```

profile of v0, /device:TPU:1, one launch (start us, length us, event | category | flops | bytes accessed | tf_op | source)
XLA Modules:
  0.0 582.6 jit_solution(2406794218687490742)
XLA Ops:
  10.8 30.1 %all-reduce.2 = (s32[192]{0:T(256)S(1)}, s32[192]{0:T(256)S(1)}) all-reduce(s32[192]{0:T(256)S(1)} %dynamic-update-slice, s32[192]{0:T(256)S(1)} %dynamic-update-slice.1), channel_id=1, replica_groups=mesh['seq'=64,'kvh'=8] {'seq'}, use_global_device_ids=true, to_apply=%add | all-reduce | flops 384 | bytes 3072
  41.1 105.8 %all-gather.3.cloned.1.call-done = bf16[192,4,1024]{2,1,0:T(4,128)(2,1)} async-done(((bf16[3,4,1024]{2,1,0:T(4,128)(2,1)}), bf16[192,4,1024]{2,1,0:T(4,128)(2,1)}) %all-gather.3.cloned.1.call-update) | async-done | bytes 1572880 | tf_op jit(solution)/shard_map/all_gather | solution.py:74
  146.9 3.6 reshape.284
  150.6 50.2 %while.14 = (s32[]{:T(128)}, f32[12,16,4,1,8]{4,2,1,3,0:T(4,128)S(1)}, f32[12,16,4,1,8]{4,2,1,3,0:T(4,128)S(1)}, f32[12,16,4,1,8,128]{5,4,2,1,3,0:T(8,128)}, s32...) while((s32[]{:T(128)}, ...), condition=%wide.region_3.4_spmd, body=%wide.region_0.3_spmd.sunk | while | flops 34146480 | bytes 4479613 | solution.py:95
  151.3 1.4 fusion.58
  155.5 1.4 fusion.58
  159.7 1.4 fusion.58
  163.9 1.4 fusion.58
  168.1 1.4 fusion.58
  172.3 1.4 fusion.58
  176.5 1.4 fusion.58
  180.6 1.4 fusion.58
  184.8 1.4 fusion.58
  189.0 1.4 fusion.58
  193.2 1.4 fusion.58
  200.8 26.9 %all_to_all.15 = f32[192,4,1,8]{3,1,2,0:T(4,128)} all-to-all(f32[192,4,1,8]{3,1,2,0:T(4,128)S(1)} %bitcast.141), channel_id=1, replica_groups=mesh['seq'=64,'kvh'=8] {'seq'}, dimensions={0} | all-to-all | bytes 49152 | tf_op jit(solution)/shard_map/all_to_all | solution.py:100
  227.7 24.4 %all_to_all.16 = f32[192,4,1,8]{3,1,2,0:T(4,128)} all-to-all(f32[192,4,1,8]{3,1,2,0:T(4,128)S(1)} %bitcast.142), channel_id=1, replica_groups=mesh['seq'=64,'kvh'=8] {'seq'}, dimensions={0} | all-to-all | bytes 49152 | tf_op jit(solution)/shard_map/all_to_all | solution.py:101
  252.1 6.6 %all-to-all-start = ((f32[192,4,1,8,128]{4,3,1,2,0:T(8,128)}), f32[192,4,1,8,128]{4,3,1,2,0:T(8,128)S(1)}, u32[]{:S(2)}, u32[]{:S(2)}) async-start(f32[192,4,1,8,128]{4,3,1,2,0:T(8,128)} %bitcast.139), calls=%async_computation | async-start | bytes 6291456 | tf_op jit(solution)/shard_map/all_to_all | solution.py:102
  261.6 1.8 subtract_exponential_fusion
  263.5 121.4 %all-to-all-done = f32[192,4,1,8,128]{4,3,1,2,0:T(8,128)S(1)} async-done(((f32[192,4,1,8,128]{4,3,1,2,0:T(8,128)}), f32[192,4,1,8,128]{4,3,1,2,0:T(8,128)S(1)}, u32[]{:S(2)}, u32[]{:S(2)}) %all-to-all-start) | async-done | bytes 3145760 | tf_op jit(solution)/shard_map/all_to_all | solution.py:102
  384.9 1.9 multiply_reduce_fusion
  387.7 141.8 %all-gather.5.cloned.1.call-done = bf16[192,4,1024]{2,1,0:T(4,128)(2,1)} async-done(((bf16[3,4,1024]{2,1,0:T(4,128)(2,1)}), bf16[192,4,1024]{2,1,0:T(4,128)(2,1)}) %all-gather.5.cloned.1.call-update) | async-done | bytes 1572880 | tf_op jit(solution)/shard_map/all_gather | solution.py:132
  529.5 3.1 fusion.20
  532.7 42.0 %reduce-scatter.2.cloned.1.call-done = f32[24,4,128]{2,0,1:T(8,128)} async-done(((f32[192,4,128]{2,0,1:T(8,128)}), f32[24,4,128]{2,0,1:T(8,128)}) %reduce-scatter.2.cloned.1.call-update) | async-done | bytes 49168 | tf_op jit(solution)/shard_map/reduce_scatter | solution.py:136
  (160 shorter events, 43.3 us)
Async XLA Ops:
  6.5 523.0 %copy-start = (bf16[1024,128]{1,0:T(8,128)(2,1)S(1)}, bf16[1024,128]{1,0:T(8,128)(2,1)}, u32[]{:S(2)}) copy-start(bf16[1024,128]{1,0:T(8,128)(2,1)} %param.17) | copy-start | bytes 786436
  6.5 144.0 %copy-start.1 = (bf16[16,128,128]{2,1,0:T(8,128)(2,1)S(1)}, bf16[16,128,128]{2,1,0:T(8,128)(2,1)}, u32[]{:S(2)}) copy-start(bf16[16,128,128]{2,1,0:T(8,128)(2,1)} %param.13) | copy-start | bytes 1572868
  6.5 144.0 %copy-start.2 = (bf16[16,128,128]{2,1,0:T(8,128)(2,1)S(1)}, bf16[16,128,128]{2,1,0:T(8,128)(2,1)}, u32[]{:S(2)}) copy-start(bf16[16,128,128]{2,1,0:T(8,128)(2,1)} %param.14) | copy-start | bytes 1572868
  6.5 140.4 %all-gather.3.cloned.1.call-start = ((), (), s32[]{:S(2)}) async-start(), calls=%async_computation.4 | async-start | bytes 1597440 | tf_op jit(solution)/shard_map/all_gather | solution.py:74
  252.1 6.7 %copy-start.3 = (bf16[3,4,1024]{2,1,0:T(4,128)(2,1)S(1)}, bf16[3,4,1024]{2,1,0:T(4,128)(2,1)}, u32[]{:S(2)}) copy-start(bf16[3,4,1024]{2,1,0:T(4,128)(2,1)} %param.10) | copy-start | bytes 73732
  252.1 6.7 %copy-start.4 = (bf16[3,4,128]{2,1,0:T(4,128)(2,1)S(1)}, bf16[3,4,128]{2,1,0:T(4,128)(2,1)}, u32[]{:S(2)}) copy-start(bf16[3,4,128]{2,1,0:T(4,128)(2,1)} %param.11) | copy-start | bytes 9220
  252.1 132.8 %all-to-all-start = ((f32[192,4,1,8,128]{4,3,1,2,0:T(8,128)}), f32[192,4,1,8,128]{4,3,1,2,0:T(8,128)S(1)}, u32[]{:S(2)}, u32[]{:S(2)}) async-start(f32[192,4,1,8,128]{4,3,1,2,0:T(8,128)} %bitcast.139), calls=%async_computation | async-start | bytes 6291456 | tf_op jit(solution)/shard_map/all_to_all | solution.py:102
  258.7 128.0 %copy-start.5 = (bf16[3,4,128]{2,1,0:T(4,128)(2,1)S(1)}, bf16[3,4,128]{2,1,0:T(4,128)(2,1)}, u32[]{:S(2)}) copy-start(bf16[3,4,128]{2,1,0:T(4,128)(2,1)} %param.12) | copy-start | bytes 9220
  258.8 270.8 %all-gather.5.cloned.1.call-start = ((), (), s32[]{:S(2)}) async-start(), calls=%async_computation.5 | async-start | bytes 1597440 | tf_op jit(solution)/shard_map/all_gather | solution.py:132
  387.7 186.9 %reduce-scatter.2.cloned.1.call-start = ((), (), s32[]{:S(2)}) async-start(), calls=%async_computation.6 | async-start | bytes 442368 | tf_op jit(solution)/shard_map/reduce_scatter | solution.py:136
Sparse Core Ops, SparseCore 0:
  10.3 136.5 all-gather.2
  387.8 141.6 all-gather.4
  532.8 41.7 reduce-scatter.1
where the time goes:
time: 584 us; the launch traced here: 583 us
  waiting for transfers between devices  412 us (71%)
  blocking collectives  81.4 us (14%)
  matrix products  32.5 us (6%)
  local copies, waits for them, and re-layouts  23.9 us (4%)
  between operations  13.8 us (2%)
  other arithmetic  11.7 us (2%)
  starting transfers between devices  6.71 us (1%)
    all_gather x1, waiting for transfers between devices, shards(): row_piece = lax.all_gather(attention, 'seq', axis=0, tiled=True)  142 us
    all_to_all x1, waiting for transfers between devices, prefix_attend(): lax.all_to_all(mix_parts, 'seq', split_axis=0, concat_axis=0, tiled=True)  121 us
    all_gather x1, waiting for transfers between devices, prefix_attend(): lax.all_gather(query_part, 'seq', axis=0, tiled=True)  106 us
    reduce_scatter x1, waiting for transfers between devices, shards(): summed = lax.psum_scatter(projected, 'kvh', scatter_dimension=0, tiled=True)  42 us
    unnamed x1, blocking collectives  30.1 us
    all_to_all x1, blocking collectives, prefix_attend(): lax.all_to_all(peak_parts, 'seq', split_axis=0, concat_axis=0, tiled=True)  26.9 us
    all_to_all x1, blocking collectives, prefix_attend(): lax.all_to_all(sum_parts, 'seq', split_axis=0, concat_axis=0, tiled=True)  24.4 us
    dot_general x12, matrix products, block_partial(): jnp.einsum('rshgd,rthd->rshgt', query_block, key_block, preferred_element...  16.6 us
  transfers between devices with their start and end apart: 4, of which 4 were waited for; matrix products, arithmetic and copies ran while one was open for 1% of the time, Pallas kernels for 0%

commit v1 on v0

v1 whole, which is shorter than its diff:
```python
import functools
import math

import jax
import jax.numpy as jnp
from jax import lax
from jax.experimental import pallas as pl
from jax.experimental.pallas import tpu as pltpu
from jax.sharding import PartitionSpec as P

HD = 128
STEPS = 4
GROUP = 8
MESH = pl.DeviceIdType.MESH
masked_score = -1e30


def kernel(
    ny, nz, nk,
    q_ref, nk_ref, nv_ref, doc_ref, len_ref, k_hbm, v_hbm, w_hbm,
    out_ref,
    kbuf, vbuf, wbuf, qf, qg, idg, ids_s, own_a, own_l,
    ya, yl, ys, yst, yr, yrt, zs, zst, zr, zrt, ag, fs, ms, part, er,
    load_sem, ids_sem, idy_send, idy_recv,
    a_send, a_recv, i_send, i_recv, ay_send, ay_recv,
    cm_send, cm_recv, cl_send, cl_recv, zm_send, zm_recv, zl_send, zl_recv,
    d_send, d_recv, dy_send, dy_recv, e_send, e_recv,
):
    seq, kv = lax.axis_index("seq"), lax.axis_index("kvh")
    y, z = lax.div(seq, nz), lax.rem(seq, nz)
    rows = q_ref.shape[0]
    vec = STEPS * GROUP
    pairs = rows * STEPS
    size = rows * vec
    steps = nz // 2
    tok = k_hbm.shape[1]
    scale = 1.0 / math.sqrt(HD)

    def at(yy, zz):
        return (lax.rem(yy + ny, ny) * nz + lax.rem(zz + nz, nz), kv)

    right, left = at(y, z + 1), at(y, z - 1)

    def peer(j):
        return at(y + j, z)

    def remote(src, dst, ssem, rsem, dev):
        return pltpu.make_async_remote_copy(
            src_ref=src, dst_ref=dst, send_sem=ssem, recv_sem=rsem,
            device_id=dev, device_id_type=MESH,
        )

    barrier = pltpu.get_barrier_semaphore()
    for j in range(1, ny):
        pl.semaphore_signal(barrier, inc=1, device_id=peer(j), device_id_type=MESH)
    for c in range(1, nz):
        pl.semaphore_signal(barrier, inc=1, device_id=at(y, z + c), device_id_type=MESH)
    for c in range(1, nk):
        pl.semaphore_signal(
            barrier, inc=1, device_id=(seq, lax.rem(kv + c, nk)), device_id_type=MESH
        )

    loads = [
        pltpu.make_async_copy(k_hbm, kbuf, load_sem.at[0]),
        pltpu.make_async_copy(v_hbm, vbuf, load_sem.at[1]),
        pltpu.make_async_copy(w_hbm, wbuf, load_sem.at[2]),
    ]
    for load in loads:
        load.start()

    for r in range(rows):
        for h in range(GROUP):
            qf[pl.ds(r * vec + h, STEPS, stride=GROUP), :] = q_ref[
                r, :, h * HD:(h + 1) * HD
            ].astype(jnp.float32)
    qg[0, 0] = qf[...].astype(jnp.bfloat16)
    lane1 = lax.broadcasted_iota(jnp.int32, (1, HD), 1)
    own_ids = jnp.zeros((1, HD), jnp.int32)
    for r in range(rows):
        own_ids = jnp.where(lane1 == r, doc_ref[r], own_ids)
        own_ids = jnp.where(lane1 == rows + r, len_ref[r], own_ids)
    idg[0, 0] = own_ids

    pl.semaphore_wait(barrier, (ny - 1) + (nz - 1) + (nk - 1))

    def q_right(i):
        return remote(
            qg.at[0, 2 * i], qg.at[0, 2 * i + 2], a_send.at[2 * i], a_recv.at[2 * i + 2], right
        )

    def q_left(i):
        return remote(
            qg.at[0, 2 * i - 1], qg.at[0, 2 * i + 1], a_send.at[2 * i - 1], a_recv.at[2 * i + 1], left
        )

    def q_first():
        return remote(qg.at[0, 0], qg.at[0, 1], a_send.at[nz - 1], a_recv.at[1], left)

    def id_right(i):
        return remote(idg.at[2 * i], idg.at[2 * i + 2], i_send.at[2 * i], i_recv.at[2 * i + 2], right)

    def id_left(i):
        return remote(
            idg.at[2 * i - 1], idg.at[2 * i + 1], i_send.at[2 * i - 1], i_recv.at[2 * i + 1], left
        )

    def id_first():
        return remote(idg.at[0], idg.at[1], i_send.at[nz - 1], i_recv.at[1], left)

    def id_peer(j):
        return remote(
            idg.at[0, 0], idg.at[0, ny - j], idy_send.at[j], idy_recv.at[ny - j], peer(j)
        )

    def q_peer(i, j):
        return remote(
            qg.at[0, pl.ds(2 * i, 2)], qg.at[ny - j, pl.ds(2 * i, 2)],
            ay_send.at[i, j], ay_recv.at[i, ny - j], peer(j),
        )

    def ids_local(i):
        return pltpu.make_async_copy(
            idg.at[pl.ds(2 * i, 2)], ids_s.at[pl.ds(2 * i, 2)], ids_sem.at[i]
        )

    q_right(0).start()
    q_first().start()
    for j in range(1, ny):
        id_peer(j).start()

    step_of = lax.broadcasted_iota(jnp.int32, (vec, 1), 0) // GROUP
    lane8 = lax.broadcasted_iota(jnp.int32, (GROUP, HD), 1)
    stats = jnp.full((GROUP, HD), masked_score, jnp.float32)
    for r in range(rows):
        q = qf[r * vec:(r + 1) * vec, :]
        keys = nk_ref[r].astype(jnp.float32)
        values = nv_ref[r].astype(jnp.float32)
        scores = []
        for t in range(STEPS):
            score = jnp.sum(q * keys[t:t + 1, :], axis=1, keepdims=True) * scale
            scores.append(jnp.where(step_of >= t, score, masked_score))
        peak = scores[0]
        for t in range(1, STEPS):
            peak = jnp.maximum(peak, scores[t])
        total = jnp.zeros((vec, 1), jnp.float32)
        mix = jnp.zeros((vec, HD), jnp.float32)
        for t in range(STEPS):
            weight = jnp.where(step_of >= t, jnp.exp(scores[t] - peak), 0.0)
            total = total + weight
            mix = mix + weight.astype(jnp.bfloat16).astype(jnp.float32) * values[t:t + 1, :]
        own_a[r * vec:(r + 1) * vec, :] = mix / total
        lse = peak + jnp.log(total)
        for s in range(STEPS):
            stats = jnp.where(
                lane8 == r * STEPS + s, lse[s * GROUP:(s + 1) * GROUP, :], stats
            )
    own_l[...] = stats

    for j in range(1, ny):
        id_peer(ny - j).wait_recv()
    id_right(0).start()
    id_first().start()
    for load in loads:
        load.wait()

    places = seq * tok + lax.broadcasted_iota(jnp.int32, (1, tok), 1)

    def attend(j, c, write):
        packed = jnp.full((GROUP, HD), masked_score, jnp.float32)
        for r in range(rows):
            doc = ids_s[c, j, 0, r]
            length = ids_s[c, j, 0, rows + r]
            q = qg[j, c, r * vec:(r + 1) * vec, :]
            scores = lax.dot_general(
                q, kbuf[doc], (((1,), (1,)), ((), ())), preferred_element_type=jnp.float32
            ) * scale
            visible = places < length
            scores = jnp.where(visible, scores, masked_score)
            peak = jnp.max(scores, axis=1, keepdims=True)
            weights = jnp.where(visible, jnp.exp(scores - peak), 0.0)
            total = jnp.sum(weights, axis=1, keepdims=True)
            mix = jnp.dot(
                weights.astype(jnp.bfloat16), vbuf[doc], preferred_element_type=jnp.float32
            )
            seen = total > 0.0
            safe = jnp.where(seen, total, 1.0)
            write(slice(r * vec, (r + 1) * vec), mix / safe)
            lse = jnp.where(seen, peak + jnp.log(safe), masked_score)
            for s in range(STEPS):
                packed = jnp.where(
                    lane8 == r * STEPS + s, lse[s * GROUP:(s + 1) * GROUP, :], packed
                )
        return packed

    def y_mix(i, j):
        return remote(
            ys.at[j - 1, pl.ds(2 * i, 2)], yr.at[ny - j - 1, pl.ds(2 * i, 2)],
            cm_send.at[i, j], cm_recv.at[i, ny - j], peer(j),
        )

    def y_lse(i, j):
        return remote(
            yst.at[j - 1, pl.ds(2 * i, 2)], yrt.at[ny - j - 1, pl.ds(2 * i, 2)],
            cl_send.at[i, j], cl_recv.at[i, ny - j], peer(j),
        )

    def z_dev(c):
        i = lax.div(c, 2)
        return at(y, jnp.where(lax.rem(c, 2) == 0, z - i, z + i + 1))

    def z_mix(c):
        return remote(zs.at[c], zr.at[c], zm_send.at[c], zm_recv.at[c], z_dev(c))

    def z_lse(c):
        return remote(zst.at[c], zrt.at[c], zl_send.at[c], zl_recv.at[c], z_dev(c))

    def merge(parts, lses):
        top = lses[0]
        for lse in lses[1:]:
            top = jnp.maximum(top, lse)
        terms = [jnp.exp(lse - top) for lse in lses]
        total = terms[0]
        for term in terms[1:]:
            total = total + term
        factors = [term / total for term in terms]

        def rows_at(k):
            result = None
            for load_part, factor in zip(parts, factors):
                wide = jnp.concatenate(
                    [
                        jnp.broadcast_to(factor[:, 2 * k:2 * k + 1], (GROUP, HD)),
                        jnp.broadcast_to(factor[:, 2 * k + 1:2 * k + 2], (GROUP, HD)),
                    ],
                    axis=0,
                )
                term = load_part(slice(16 * k, 16 * k + 16)).astype(jnp.float32) * wide
                result = term if result is None else result + term
            return result

        return rows_at, top + jnp.log(total)

    def stage_a(i):
        @pl.when(i > 0)
        def _():
            q_right(i - 1).wait_recv()
            id_right(i - 1).wait_recv()

            @pl.when(i < steps - 1)
            def _():
                q_right(i).start()
                id_right(i).start()

        @pl.when(i == 0)
        def _():
            q_first().wait_recv()
            id_first().wait_recv()

        @pl.when(i > 0)
        def _():
            q_left(i).wait_recv()
            id_left(i).wait_recv()

        @pl.when(i < steps - 1)
        def _():
            q_left(i + 1).start()
            id_left(i + 1).start()

        for j in range(1, ny):
            q_peer(i, j).start()
        ids_local(i).start()

    def stage_b(i):
        ids_local(i).wait()
        for j in range(1, ny):
            q_peer(i, ny - j).wait_recv()

        @pl.loop(0, 2)
        def _(cc):
            c = 2 * i + cc
            for j in range(ny):
                if j == 0:
                    def write(where, value):
                        ya[c, where, :] = value

                    yl[c] = attend(j, c, write)
                else:
                    def write(where, value, j=j):
                        ys[j - 1, c, where, :] = value.astype(jnp.bfloat16)

                    yst[j - 1, c] = attend(j, c, write)

        for j in range(1, ny):
            y_mix(i, j).start()
            y_lse(i, j).start()

    def stage_c(i):
        for j in range(1, ny):
            y_mix(i, ny - j).wait_recv()
            y_lse(i, ny - j).wait_recv()

        @pl.loop(0, 2)
        def _(cc):
            c = 2 * i + cc
            parts = [lambda where: ya[c, where, :]]
            lses = [yl[c]]
            for j in range(1, ny):
                parts.append(lambda where, j=j: yr[j - 1, c, where, :])
                lses.append(yrt[j - 1, c])
            rows_at, lse = merge(parts, lses)
            for k in range(size // 16):
                zs[c, 16 * k:16 * k + 16, :] = rows_at(k).astype(jnp.bfloat16)
            zst[c] = lse

            @pl.when(c > 0)
            def _():
                z_mix(c).start()
                z_lse(c).start()

    @pl.loop(0, steps + 2)
    def _(i):
        @pl.when(i < steps)
        def _():
            stage_a(i)

        @pl.when(jnp.logical_and(i >= 1, i < steps + 1))
        def _():
            stage_b(i - 1)

        @pl.when(i >= 2)
        def _():
            stage_c(i - 2)

    @pl.loop(1, nz)
    def _(c):
        z_mix(c).wait_recv()
        z_lse(c).wait_recv()

    parts = [lambda where: own_a[where, :], lambda where: zs[0, where, :]]
    lses = [own_l[...], zst[0]]
    for c in range(1, nz):
        parts.append(lambda where, c=c: zr[c, where, :])
        lses.append(zrt[c])
    rows_at, _ = merge(parts, lses)
    for k in range(size // 16):
        ag[0, 0, 16 * k:16 * k + 16, :] = rows_at(k).astype(jnp.bfloat16)

    def d_right(i):
        return remote(
            ag.at[0, 2 * i], ag.at[0, 2 * i + 2], d_send.at[2 * i], d_recv.at[2 * i + 2], right
        )

    def d_left(i):
        return remote(
            ag.at[0, 2 * i - 1], ag.at[0, 2 * i + 1], d_send.at[2 * i - 1], d_recv.at[2 * i + 1], left
        )

    def d_first():
        return remote(ag.at[0, 0], ag.at[0, 1], d_send.at[nz - 1], d_recv.at[1], left)

    def d_peer(i, j):
        return remote(
            ag.at[0, pl.ds(2 * i, 2)], ag.at[ny - j, pl.ds(2 * i, 2)],
            dy_send.at[i, j], dy_recv.at[i, ny - j], peer(j),
        )

    d_right(0).start()
    d_first().start()

    def gather(i):
        @pl.when(i > 0)
        def _():
            d_right(i - 1).wait_recv()

            @pl.when(i < steps - 1)
            def _():
                d_right(i).start()

        @pl.when(i == 0)
        def _():
            d_first().wait_recv()

        @pl.when(i > 0)
        def _():
            d_left(i).wait_recv()

        @pl.when(i < steps - 1)
        def _():
            d_left(i + 1).start()

        for j in range(1, ny):
            d_peer(i, j).start()

    def project(i):
        for j in range(1, ny):
            d_peer(i, ny - j).wait_recv()
        for cc in range(2):
            for j in range(ny):
                first = (cc * ny + j) * size
                fs[first:first + size, :] = ag[j, 2 * i + cc].astype(jnp.float32)
        total = None
        for h in range(GROUP):
            piece = fs[pl.ds(h, 2 * ny * pairs, stride=GROUP), :].astype(jnp.bfloat16)
            term = jnp.dot(
                piece, wbuf[h * HD:(h + 1) * HD, :], preferred_element_type=jnp.float32
            )
            total = term if total is None else total + term
        ms[...] = total
        for cc in range(2):
            column = lax.rem((z - i if cc == 0 else z + i + 1) + nz, nz)
            for j in range(ny):
                owner = lax.rem(y + j, ny) * nz + column
                first = (cc * ny + j) * pairs
                part[owner] = ms[first:first + pairs, :]

    @pl.loop(0, steps + 1)
    def _(i):
        @pl.when(i < steps)
        def _():
            gather(i)

        @pl.when(i >= 1)
        def _():
            project(i - 1)

    blocks = ny * nz // nk

    def e_copy(c):
        other = lax.rem(kv + c, nk)
        return remote(
            part.at[pl.ds(other * blocks, blocks)], er.at[nk - c],
            e_send.at[c], e_recv.at[nk - c], (seq, other),
        )

    for c in range(1, nk):
        e_copy(c).start()
    for c in range(1, nk):
        e_copy(nk - c).wait_recv()
    result = part[pl.ds(kv * blocks, blocks)]
    for c in range(1, nk):
        result = result + er[c]
    out_ref[...] = result.astype(out_ref.dtype)

    q_first().wait_send()
    id_first().wait_send()
    d_first().wait_send()

    @pl.loop(0, steps - 1)
    def _(i):
        q_right(i).wait_send()
        id_right(i).wait_send()
        d_right(i).wait_send()
        q_left(i + 1).wait_send()
        id_left(i + 1).wait_send()
        d_left(i + 1).wait_send()

    for j in range(1, ny):
        id_peer(j).wait_send()

    @pl.loop(0, steps)
    def _(i):
        for j in range(1, ny):
            q_peer(i, j).wait_send()
            y_mix(i, j).wait_send()
            y_lse(i, j).wait_send()
            d_peer(i, j).wait_send()

    @pl.loop(1, nz)
    def _(c):
        z_mix(c).wait_send()
        z_lse(c).wait_send()

    for c in range(1, nk):
        e_copy(c).wait_send()


def solution(mesh, ny=None):
    nseq, nk = mesh.shape["seq"], mesh.shape["kvh"]
    ny = 4 if ny is None else ny
    nz = nseq // ny
    steps = nz // 2

    def shards(queries, new_keys, new_values, key_cache, value_cache, doc_ids, prefix_len, out_weight):
        rows = queries.shape[0]
        size = rows * STEPS * GROUP
        pairs = rows * STEPS
        blocks = nseq // nk
        bf, f32 = jnp.bfloat16, jnp.float32
        vmem = pl.BlockSpec(memory_space=pltpu.VMEM)
        smem = pl.BlockSpec(memory_space=pltpu.SMEM)
        anyw = pl.BlockSpec(memory_space=pl.ANY)
        dma = pltpu.SemaphoreType.DMA
        result = pl.pallas_call(
            functools.partial(kernel, ny, nz, nk),
            out_shape=jax.ShapeDtypeStruct((blocks, pairs, HD), bf),
            in_specs=[vmem, vmem, vmem, smem, smem, anyw, anyw, anyw],
            out_specs=vmem,
            scratch_shapes=[
                pltpu.VMEM(key_cache.shape, bf),
                pltpu.VMEM(value_cache.shape, bf),
                pltpu.VMEM(out_weight.shape, bf),
                pltpu.VMEM((size, HD), f32),
                pltpu.VMEM((ny, nz, size, HD), bf),
                pltpu.VMEM((nz, ny, 1, HD), jnp.int32),
                pltpu.SMEM((nz, ny, 1, HD), jnp.int32),
                pltpu.VMEM((size, HD), f32),
                pltpu.VMEM((GROUP, HD), f32),
                pltpu.VMEM((nz, size, HD), f32),
                pltpu.VMEM((nz, GROUP, HD), f32),
                pltpu.VMEM((ny - 1, nz, size, HD), bf),
                pltpu.VMEM((ny - 1, nz, GROUP, HD), f32),
                pltpu.VMEM((ny - 1, nz, size, HD), bf),
                pltpu.VMEM((ny - 1, nz, GROUP, HD), f32),
                pltpu.VMEM((nz, size, HD), bf),
                pltpu.VMEM((nz, GROUP, HD), f32),
                pltpu.VMEM((nz, size, HD), bf),
                pltpu.VMEM((nz, GROUP, HD), f32),
                pltpu.VMEM((ny, nz, size, HD), bf),
                pltpu.VMEM((2 * ny * size, HD), f32),
                pltpu.VMEM((2 * ny * pairs, HD), f32),
                pltpu.VMEM((nseq, pairs, HD), f32),
                pltpu.VMEM((nk, blocks, pairs, HD), f32),
                dma((3,)), dma((steps,)), dma((ny,)), dma((ny,)),
                dma((nz,)), dma((nz,)), dma((nz,)), dma((nz,)),
                dma((steps, ny)), dma((steps, ny)),
                dma((steps, ny)), dma((steps, ny)), dma((steps, ny)), dma((steps, ny)),
                dma((nz,)), dma((nz,)), dma((nz,)), dma((nz,)),
                dma((nz,)), dma((nz,)), dma((steps, ny)), dma((steps, ny)),
                dma((nk,)), dma((nk,)),
            ],
            compiler_params=pltpu.CompilerParams(
                collective_id=0, has_side_effects=True, vmem_limit_bytes=40 * 1024 * 1024
            ),
        )(queries, new_keys, new_values, doc_ids, prefix_len, key_cache, value_cache, out_weight)
        return result.reshape(nseq * rows // nk, STEPS, HD)

    return jax.shard_map(
        shards,
        mesh=mesh,
        in_specs=(
            P("seq", None, "kvh"),
            P("seq", None, "kvh"),
            P("seq", None, "kvh"),
            P(None, "seq", "kvh"),
            P(None, "seq", "kvh"),
            P("seq"),
            P("seq"),
            P("kvh", "seq"),
        ),
        out_specs=P("kvh", None, "seq"),
        check_vma=False,
    )
```

time: 584 us -> 139 us (0.24)
  waiting for transfers between devices: 412 us -> 0 us
  Pallas kernels: 0 us -> 131 us
  blocking collectives: 81.4 us -> 0 us
  matrix products: 32.5 us -> 0 us
  local copies, waits for them, and re-layouts: 23.9 us -> 7.07 us
  between operations: 13.8 us -> 0.02 us
  other arithmetic: 11.7 us -> 0 us
  starting transfers between devices: 6.71 us -> 0 us
    all_gather x2 -> x0, waiting for transfers between devices: 248 us -> none  [the longest x1 142 us: shards(): row_piece = lax.all_gather(attention, 'seq', axis=0, tiled=True)]
    pallas_call x0 -> x1, Pallas kernels: none -> 131 us  [shards(): pl.pallas_call(functools.partial(kernel, ny, nz, nk), out_shape=jax.Shape...]
    all_to_all x1 -> x0, waiting for transfers between devices: 121 us -> none  [prefix_attend(): lax.all_to_all(mix_parts, 'seq', split_axis=0, concat_axis=0, tiled=True)]
    all_to_all x2 -> x0, blocking collectives: 51.3 us -> none  [the longest x1 26.9 us: prefix_attend(): lax.all_to_all(peak_parts, 'seq', split_axis=0, concat_axis=0, tiled=True)]
    reduce_scatter x1 -> x0, waiting for transfers between devices: 42 us -> none  [shards(): summed = lax.psum_scatter(projected, 'kvh', scatter_dimension=0, tiled=True)]
    dot_general x27 -> x0, matrix products: 32.5 us -> none  [the longest x12 16.6 us: block_partial(): jnp.einsum('rshgd,rthd->rshgt', query_block, key_block, preferred_element...]
    unnamed x1 -> x0, blocking collectives: 30.1 us -> none
    gather x24 -> x0, local copies, waits for them, and re-layouts: 15.5 us -> none  [the longest x12 7.77 us: one_block(): key_cache[doc_block].reshape(block_rows, tok_block, heads_kv, HD)]
  transfers between devices with their start and end apart: 4 -> 0, of which waited for: 4 -> 0; matrix products, arithmetic and copies ran while one was open for 1% -> 0% of each run, Pallas kernels for 0% -> 0%
where the time goes in v1:
time: 139 us
  Pallas kernels  131 us (94%)
  local copies, waits for them, and re-layouts  7.07 us (5%)
    pallas_call x1, Pallas kernels, shards(): pl.pallas_call(functools.partial(kernel, ny, nz, nk), out_shape=jax.Shape...  131 us
    unnamed x16, local copies, waits for them, and re-layouts  6.45 us

profile of v1, /device:TPU:1, one launch (start us, length us, event | category | flops | bytes accessed | tf_op | source)
XLA Modules:
  0.0 138.5 jit_solution(12472790899355349121)
XLA Ops:
  0.0 0.0 copy-start
  0.0 1.0 copy-done
  1.0 0.0 copy-start.1
  1.0 1.0 copy-done.1
  2.1 0.0 copy-start.2
  2.1 0.9 copy-done.2
  3.0 0.0 copy-start.3
  3.0 0.7 copy-done.3
  3.8 0.0 copy-start.4
  3.8 0.7 copy-done.4
  4.5 0.0 copy-start.5
  4.5 0.7 copy-done.5
  5.1 0.0 copy-start.6
  5.1 0.7 copy-done.6
  5.8 0.0 copy-start.7
  5.8 0.7 copy-done.7
  6.5 131.4 %shard_map.82 = bf16[8,12,128]{2,1,0:T(8,128)(2,1)S(1)} custom-call(bf16[3,4,1024]{2,1,0:T(4,128)(2,1)S(1)} %copy-done.3, bf16[3,4,128]{2,1,0:T(4,128)(2,1)S(1)} %copy-done.4, bf16[3,4,128]{2,1,0:T(4,128)(2,1)S(1)} %copy-done.5, s32[3]{0:T(128)S(1)} %copy-done.6, s32[3]{0:T(128)S(1)} %copy-done.7, bf16[16,128,128]{2,1,0:T(8,128)(2,1)S(1)} %copy-done, ...), custom_call_target="tpu_custom_call" | custom-call | tf_op jit(solution)/shard_map/pallas_call | solution.py:493
  137.9 0.6 reshape.3
Async XLA Ops:
  0.0 1.0 copy-start
  1.0 1.0 copy-start.1
  2.1 0.9 copy-start.2
  3.0 0.7 copy-start.3
  3.8 0.7 copy-start.4
  4.5 0.7 copy-start.5
  5.1 0.7 copy-start.6
  5.8 0.7 copy-start.7
